TPU v7x, 32 devices: a whole 2x2x4 slice. The times are simulated.
32 devices in a mesh: grp: 2 (over y), slab: 4 (over z), mem: 2 (over x), sub: 2 (over core).
Axes of the slice: x: 2, y: 2, z: 4, core: 2. Of those that a mesh axis runs over, the one named last changes fastest.
Arguments:
- state: bfloat16 [256, 32768], P('mem', ('grp', 'slab', 'sub')), parts along dimension 1, may hold values from -6 to 6
- centers: int32 [512], P('grp'), parts along dimension 0, may hold values from 0 to 16383, as said below
- half_width: int32 [512], P('grp'), parts along dimension 0, may hold values from 4 to 71
- radius: int32 [512], P('grp'), parts along dimension 0, may hold values from 2048 to 8192
- order: int32 [512], P('grp'), parts along dimension 0, may hold values from 0 to 255, each once
- obs_var: float32 [512], P('grp'), parts along dimension 0, may hold values from 0.1 to 1
Outputs:
- analysis: bfloat16 [256, 32768], P('mem', ('grp', 'slab', 'sub')), parts along dimension 1
There are 2 independent parts, one for each index of `grp`. A program takes and returns all parts, laid end to end along the dimension named above; each array names one. Nothing has to cross between parts.
Inputs may be any that keep to these rules, and one draw needn't show every extreme that they name: order holds every observation number once. Observations 4 k to 4 k + 3 have centers within 6 rows of a common site row, which the first of them sits on; centers are clipped to the grid.
All inputs are finite; a program needn't handle non-finite values.
Results may differ from a plain program's by a relative error of at most 0.0049.
Values may be sent and summed in bfloat16 or wider, within the bound.
A program may use at most 64 MiB of HBM per device.

v0:
```python
import math

import jax
import jax.numpy as jnp
from jax import lax
from jax.sharding import PartitionSpec as P

M = 256
P_SIZE = 128
BATCHES = 2


floor_level = math.exp(-2.0)


def geometry(first_row, row_count, center_rows, half_rows, radius_rows):
    rows_all = first_row + lax.iota(jnp.int32, row_count)
    distance = (rows_all[None, :] - center_rows[:, None]).astype(jnp.float32)
    half_f = half_rows.astype(jnp.float32)[:, None]
    footprint = (
        jnp.maximum(jnp.exp(-2.0 * distance * distance / (half_f * half_f)) - floor_level, 0.0)
        / jnp.sqrt(half_f)
    ).astype(jnp.bfloat16)
    taper_rows = jnp.square(
        jnp.maximum(1.0 - jnp.abs(distance) / radius_rows.astype(jnp.float32)[:, None], 0.0)
    )
    return (footprint, taper_rows)


def gain_terms(projected, variance):
    high = lax.Precision.HIGHEST
    covariance = jnp.dot(
        projected.T, projected, precision=high, preferred_element_type=jnp.float32
    ) / (M - 1) + jnp.diag(variance)
    factor = jnp.linalg.cholesky(covariance)
    identity = jnp.eye(P_SIZE, dtype=jnp.float32)
    inner_inv = lax.linalg.triangular_solve(
        factor + jnp.diag(jnp.sqrt(variance)), identity, left_side=True, lower=True
    )
    gain_mat = lax.linalg.triangular_solve(
        factor, inner_inv, left_side=True, lower=True, transpose_a=True
    )
    weights = jnp.dot(
        projected, gain_mat.T, precision=high, preferred_element_type=jnp.float32
    ).astype(jnp.bfloat16)
    return (weights, projected.astype(jnp.bfloat16))


def project_rows(ensemble, footprint):
    return lax.dot_general(
        ensemble, footprint, (((1,), (1,)), ((), ())), preferred_element_type=jnp.float32
    )


def cross_rows(projected_b, ensemble):
    return lax.dot_general(
        projected_b, ensemble, (((0,), (0,)), ((), ())), preferred_element_type=jnp.float32
    )


def on_device(state, centers, half_width, radius, order, obs_var):
    own_count, rows_here = state.shape
    row_base = lax.axis_index(("slab", "sub")) * rows_here
    centers_all = centers[order]
    half_all = half_width[order]
    radius_all = radius[order]
    variance_all = obs_var[order]
    ensemble = state
    offset = lax.axis_index("mem") * own_count
    for batch in range(BATCHES):
        lo_obs = batch * P_SIZE
        footprint, taper_rows = geometry(
            row_base,
            rows_here,
            centers_all[lo_obs : lo_obs + P_SIZE],
            half_all[lo_obs : lo_obs + P_SIZE],
            radius_all[lo_obs : lo_obs + P_SIZE],
        )
        partial_value = project_rows(ensemble, footprint)
        summed_own = lax.psum(partial_value, ("slab", "sub"))
        projected = lax.all_gather(summed_own, "mem", axis=0, tiled=True)
        weights, projected_b = gain_terms(projected, variance_all[lo_obs : lo_obs + P_SIZE])
        cross_cov = cross_rows(projected_b, lax.all_gather(ensemble, "mem", axis=0, tiled=True))
        tapered = (taper_rows * cross_cov / (M - 1)).astype(jnp.bfloat16)
        weights_own = lax.dynamic_slice_in_dim(weights, offset, own_count, 0)
        ensemble = (
            ensemble.astype(jnp.float32)
            - jnp.dot(weights_own, tapered, preferred_element_type=jnp.float32)
        ).astype(jnp.bfloat16)
    return ensemble


def solution(mesh):
    placed = (P("mem", ("grp", "slab", "sub")), P("grp"), P("grp"), P("grp"), P("grp"), P("grp"))
    return jax.shard_map(
        on_device,
        mesh=mesh,
        in_specs=placed,
        out_specs=P("mem", ("grp", "slab", "sub")),
        check_vma=False,
    )
```

profile of v0, /device:TPU:0, one launch (start us, length us, event | category | flops | bytes accessed | tf_op | source)
XLA Modules:
  0.0 215.7 jit_solution(16010699349236108994)
XLA Ops:
  7.4 0.7 copy-done.8
  8.1 1.9 gather_fusion.1
  10.1 0.7 copy-done.1
  10.7 1.9 gather_fusion
  12.7 1.2 convolution_bitcast_fusion
  15.2 1.9 gather_fusion.2
  17.2 0.7 copy-done.3
  17.9 1.9 gather_fusion.3
  19.8 50.6 %all-reduce.3.cloned.1.call-done = f32[128,128]{0,1:T(8,128)} async-done(((f32[128,128]{0,1:T(8,128)}), f32[128,128]{0,1:T(8,128)}) %all-reduce.3.cloned.1.call-update) | async-done | bytes 65552 | tf_op jit(solution)/shard_map/psum | solution.py:80
  70.4 5.3 %all_gather.12 = f32[256,128]{0,1:T(8,128)S(1)} all-gather(f32[128,128]{0,1:T(8,128)} %all-reduce.3.cloned.1.call-done), channel_id=1, replica_groups=mesh['grp'=2,'slab'=4,'mem'=2,'sub'=2] {'mem'}, dimensions={0}, use_global_device_ids=true | all-gather | bytes 196608 | tf_op jit(solution)/shard_map/all_gather | solution.py:81
  76.2 11.7 %cholesky.44 = f32[128,128]{1,0:T(8,128)S(1)} custom-call(f32[128,128]{1,0:T(8,128)S(1)} %copy.12), custom_call_target="Cholesky" | custom-call | tf_op jit(solution)/shard_map/jit(cholesky)/cholesky | solution.py:35
  88.6 0.7 select_bitcast_fusion.2
  89.4 9.8 %custom-call.10 = f32[1,128,128]{1,2,0:T(8,128)S(1)} custom-call(f32[1,128,128]{2,1,0:T(8,128)S(1)} %get-tuple-element.11), custom_call_target="InvertDiagBlocksLowerTriangular" | custom-call | tf_op jit(solution)/shard_map/triangular_solve/custom-call.0 | solution.py:37
  99.2 9.8 %custom-call.11 = f32[1,128,128]{1,2,0:T(8,128)S(1)} custom-call(f32[1,128,128]{2,1,0:T(8,128)S(1)} %get-tuple-element.10), custom_call_target="InvertDiagBlocksLowerTriangular" | custom-call | tf_op jit(solution)/shard_map/triangular_solve/custom-call.2 | solution.py:40
  109.9 2.0 fusion.4
  111.9 1.3 fusion.35
  113.8 52.2 %all-reduce.5.cloned.1.call-done = f32[128,128]{1,0:T(8,128)} async-done(((f32[128,128]{1,0:T(8,128)}), f32[128,128]{1,0:T(8,128)}) %all-reduce.5.cloned.1.call-update) | async-done | bytes 65552 | tf_op jit(solution)/shard_map/psum | solution.py:80
  166.0 5.4 %all_gather.14 = f32[256,128]{1,0:T(8,128)S(1)} all-gather(f32[128,128]{1,0:T(8,128)} %all-reduce.5.cloned.1.call-done), channel_id=1, replica_groups=mesh['grp'=2,'slab'=4,'mem'=2,'sub'=2] {'mem'}, dimensions={0}, use_global_device_ids=true | all-gather | bytes 196608 | tf_op jit(solution)/shard_map/all_gather | solution.py:81
  171.9 11.7 %cholesky.55 = f32[128,128]{1,0:T(8,128)S(1)} custom-call(f32[128,128]{1,0:T(8,128)S(1)} %copy.14), custom_call_target="Cholesky" | custom-call | tf_op jit(solution)/shard_map/jit(cholesky)/cholesky | solution.py:35
  183.7 0.7 compare_reduce_fusion
  184.4 0.7 select_bitcast_fusion
  185.1 9.8 %custom-call.12 = f32[1,128,128]{1,2,0:T(8,128)S(1)} custom-call(f32[1,128,128]{2,1,0:T(8,128)S(1)} %get-tuple-element.8), custom_call_target="InvertDiagBlocksLowerTriangular" | custom-call | tf_op jit(solution)/shard_map/triangular_solve/custom-call.0 | solution.py:37
  194.9 9.8 %custom-call.13 = f32[1,128,128]{1,2,0:T(8,128)S(1)} custom-call(f32[1,128,128]{2,1,0:T(8,128)S(1)} %get-tuple-element.6), custom_call_target="InvertDiagBlocksLowerTriangular" | custom-call | tf_op jit(solution)/shard_map/triangular_solve/custom-call.2 | solution.py:40
  205.5 2.8 %fusion.5 = bf16[128,2048]{1,0:T(8,128)(2,1)} fusion(bf16[256,2048]{1,0:T(8,128)(2,1)} %all-gather.5.cloned.1.call-done, bf16[128,2048]{1,0:T(8,128)(2,1)S(1)} %copy-done.7, f32[128]{0:T(128)S(1)} %get-tuple-element.22, s32[128]{0:T(128)S(1)} %get-tuple-element.20, s32[2048]{0:T(1024)S(1)} %iota_add_fusion, f32[256,128]{1,0:T(8,128)S(1)} %all_gather.14, ...), kind=kOutput, calls=%fused_computation.13 | convolution fusion | flops 204767232 | bytes 2270212 | tf_op jit(solution)/shard_map/dot_general | solution.py:88
  (49 shorter events, 5.4 us)
Async XLA Ops:
  7.4 0.7 copy-start
  7.4 63.0 %all-reduce.3.cloned.1.call-start = ((), (), s32[]{:S(2)}) async-start(), calls=%async_computation | async-start | bytes 131072 | tf_op jit(solution)/shard_map/psum | solution.py:80
  7.4 0.7 copy-start.8
  10.0 0.7 copy-start.1
  10.7 2.0 copy-start.4
  13.9 96.0 %all-gather.3.cloned.1.call-start = ((), (), s32[]{:S(2)}) async-start(), calls=%async_computation.1 | async-start | bytes 1572864 | tf_op jit(solution)/shard_map/all_gather | solution.py:83
  14.5 0.7 copy-start.2
  14.5 151.4 %all-reduce.5.cloned.1.call-start = ((), (), s32[]{:S(2)}) async-start(), calls=%async_computation.2 | async-start | bytes 131072 | tf_op jit(solution)/shard_map/psum | solution.py:80
  17.2 0.7 copy-start.3
  76.1 33.8 %copy-start.5 = (bf16[128,2048]{1,0:T(8,128)(2,1)S(1)}, bf16[128,2048]{1,0:T(8,128)(2,1)}, u32[]{:S(2)}) copy-start(bf16[128,2048]{1,0:T(8,128)(2,1)} %param.11) | copy-start | bytes 1572868
  111.9 1.3 copy-start.6
  113.2 92.3 %all-gather.5.cloned.1.call-start = ((), (), s32[]{:S(2)}) async-start(), calls=%async_computation.3 | async-start | bytes 1572864 | tf_op jit(solution)/shard_map/all_gather | solution.py:83
  171.8 33.7 %copy-start.7 = (bf16[128,2048]{1,0:T(8,128)(2,1)S(1)}, bf16[128,2048]{1,0:T(8,128)(2,1)}, u32[]{:S(2)}) copy-start(bf16[128,2048]{1,0:T(8,128)(2,1)} %copy-done.6) | copy-start | bytes 1572868
Sparse Core Ops, SparseCore 0:
  14.1 56.3 all-reduce.2
  113.3 52.5 all-reduce.4
Sparse Core Ops, SparseCore 1:
  16.0 23.9 all-gather.2
  115.3 20.2 all-gather.4
where the time goes:
time: 216 us
  waiting for transfers between devices  104 us (48%)
  other arithmetic  65.5 us (30%)
  between operations  15.2 us (7%)
  local copies, waits for them, and re-layouts  10.8 us (5%)
  blocking collectives  10.7 us (5%)
  matrix products  9.54 us (4%)
    psum x2, waiting for transfers between devices, on_device(): summed_own = lax.psum(partial_value, ('slab', 'sub'))  103 us
    another operation x6, other arithmetic, gain_terms(): factor = jnp.linalg.cholesky(covariance)  24.8 us
    another operation x4, other arithmetic, gain_terms(): lax.linalg.triangular_solve(factor, inner_inv, left_side=True, lower=True...  21 us
    another operation x2, other arithmetic, gain_terms(): lax.linalg.triangular_solve(factor + jnp.diag(jnp.sqrt(variance)), identi...  19.6 us
    all_gather x2, blocking collectives, on_device(): projected = lax.all_gather(summed_own, 'mem', axis=0, tiled=True)  10.7 us
    dot_general x2, matrix products, on_device(): jnp.dot(weights_own, tapered, preferred_element_type=jnp.float32)  4.76 us
  transfers between devices with their start and end apart: 4, of which 2 were waited for; matrix products, arithmetic and copies ran while one was open for 33% of the time, Pallas kernels for 0%

commit v1 on v0

v1 whole, which is shorter than its diff:
```python
import functools
import math

import jax
import jax.numpy as jnp
from jax import lax
from jax.experimental import pallas as pl
from jax.experimental.pallas import tpu as pltpu
from jax.sharding import PartitionSpec as P

M = 256
P_SIZE = 128
BATCHES = 2
BLOCK = 16
TILE = 256

FLOOR = math.exp(-2.0)
F32 = jnp.float32
BF16 = jnp.bfloat16
HIGH = lax.Precision.HIGHEST
LAST = (((1,), (1,)), ((), ()))
FIRST = (((0,), (0,)), ((), ()))


def each(start, stop, body):
    if stop - start <= 16:
        for i in range(start, stop):
            body(i)
    else:

        def step(i, carry):
            body(i)
            return carry

        lax.fori_loop(start, stop, step, 0)


def split3(x):
    high = x.astype(BF16)
    rest = x - high.astype(F32)
    mid = rest.astype(BF16)
    low = (rest - mid.astype(F32)).astype(BF16)
    return high, mid, low


def sweep(work, inv, solved, root):
    b = BLOCK
    width = work.shape[1] // P_SIZE

    def step(k, carry):
        r0 = pl.multiple_of(k * b, b)
        parts = [work[pl.ds(r0, b), g * P_SIZE : (g + 1) * P_SIZE] for g in range(width)]
        roots = root[pl.ds(r0, b), :]
        rolled = pltpu.roll(parts[0], lax.rem(P_SIZE - r0, P_SIZE), 1)
        cols = [jnp.broadcast_to(rolled[:, j : j + 1], (b, P_SIZE)) for j in range(b)]
        row_id = lax.broadcasted_iota(jnp.int32, (b, P_SIZE), 0)
        for j in range(b):
            pivot = cols[j][j : j + 1, :]
            scale = lax.rsqrt(pivot)
            scale_m = 1.0 / (pivot * scale + roots[j : j + 1, :])
            column = jnp.where(row_id > j, cols[j] * scale, 0.0)
            for i in range(j + 1, b):
                cols[i] = cols[i] - column * column[i : i + 1, :]
            for g in range(width):
                row = parts[g][j : j + 1, :] * (scale if g < 2 else scale_m)
                parts[g] = jnp.where(row_id == j, row, parts[g] - column * row)
        inv[pl.ds(r0, b), :] = parts[1]
        for g in range(2, width):
            solved[pl.ds(r0, b), (g - 2) * P_SIZE : (g - 1) * P_SIZE] = parts[g]
        pieces = [split3(x) for x in parts]
        h, m, l = pieces[0]
        left = jnp.concatenate([h, h, m, h, m, l], axis=0)
        h, m, l = (jnp.concatenate([x[n] for x in pieces], axis=1) for n in range(3))
        right = jnp.concatenate([h, m, h, l, m, h], axis=0)
        work[...] -= lax.dot_general(left, right, FIRST, preferred_element_type=F32)
        return carry

    lax.fori_loop(0, P_SIZE // b, step, 0)


def kernel(
    shape,
    state, cen, half, rad, order, var,
    out,
    e_all, foot, tap, col_c, col_r, var_b, root_b, work, inv, solved, wts,
    part, rs, ag, cpart, crs, cag,
    e_ss, e_rs, rs_ss, rs_rs, ag_ss, ag_rs,
):
    n_slab, n_mem, n_sub = shape
    n = n_slab * n_sub
    total = n * n_mem
    owners = min(n, 8)
    stride = n // owners
    chunk = P_SIZE // owners
    own, rows = state.shape
    n_tiles = rows // TILE

    mi = lax.axis_index("mem")
    me = lax.axis_index("slab") * n_sub + lax.axis_index("sub")
    mine = lax.div(me, stride)

    def peer(red, mem):
        return {"slab": lax.div(red, n_sub), "sub": lax.rem(red, n_sub), "mem": mem}

    def peer_of(off):
        red = lax.rem(me + lax.rem(off, n), n)
        mem = lax.rem(mi + lax.div(off, n), n_mem)
        return red, mem

    def owner_only(body):
        if stride == 1:
            body()
        else:
            pl.when(lax.rem(me, stride) == 0)(body)

    barrier = pltpu.get_barrier_semaphore()

    def greet(off):
        red, mem = peer_of(off)
        pl.semaphore_signal(
            barrier, inc=1, device_id=peer(red, mem), device_id_type=pl.DeviceIdType.MESH
        )

    each(1, total, greet)

    n_obs = BATCHES * P_SIZE
    picked = jnp.broadcast_to(order[...].astype(F32), (P_SIZE, n_obs)).T.astype(jnp.int32)
    lane = lax.broadcasted_iota(jnp.int32, (n_obs, P_SIZE), 1)
    masks = [picked == lane + h * P_SIZE for h in range(BATCHES)]

    def pick(ref):
        value = ref[...].astype(F32)
        chosen = 0.0
        for h in range(BATCHES):
            chosen = chosen + jnp.where(masks[h], value[:, h * P_SIZE : (h + 1) * P_SIZE], 0.0)
        return jnp.sum(chosen, axis=1, keepdims=True)

    center = pick(cen) - (me * rows).astype(F32)
    width = pick(half)
    variance = pick(var)
    col_c[...] = jnp.broadcast_to(center, (n_obs, P_SIZE))
    col_r[...] = jnp.broadcast_to(1.0 / pick(rad), (n_obs, P_SIZE))
    var_b[...] = jnp.broadcast_to(variance, (n_obs, P_SIZE))
    root_b[...] = jnp.broadcast_to(jnp.sqrt(variance), (n_obs, P_SIZE))
    steep = jnp.broadcast_to(-2.0 / (width * width), (n_obs, TILE))
    height = jnp.broadcast_to(1.0 / jnp.sqrt(width), (n_obs, TILE))
    center_w = jnp.broadcast_to(center, (n_obs, TILE))

    pl.semaphore_wait(barrier, total - 1)

    def e_copy(off):
        return pltpu.make_async_remote_copy(
            src_ref=state,
            dst_ref=e_all.at[mi],
            send_sem=e_ss.at[off],
            recv_sem=e_rs.at[mi],
            device_id=peer(me, lax.rem(mi + off, n_mem)),
            device_id_type=pl.DeviceIdType.MESH,
        )

    each(1, n_mem, lambda off: e_copy(off).start())
    e_all[mi] = state[...]

    def foot_tile(t, carry):
        at = pl.multiple_of(t * TILE, TILE)
        row = lax.broadcasted_iota(jnp.int32, (n_obs, TILE), 1) + at
        distance = row.astype(F32) - center_w
        shape_f = jnp.maximum(jnp.exp(distance * distance * steep) - FLOOR, 0.0) * height
        foot[:, pl.ds(at, TILE)] = shape_f.astype(BF16)
        return carry

    lax.fori_loop(0, n_tiles, foot_tile, 0)
    sums = lax.dot_general(foot[...], state[...], LAST, preferred_element_type=F32)
    for b in range(BATCHES):
        for o in range(owners):
            lo = b * P_SIZE + o * chunk
            part[b, o] = sums[lo : lo + chunk, :]

    def reduce_copy(source, target, x, off):
        o = lax.rem(mine + off, owners)
        return pltpu.make_async_remote_copy(
            src_ref=source.at[o],
            dst_ref=target.at[me],
            send_sem=rs_ss.at[x, off],
            recv_sem=rs_rs.at[x, me],
            device_id=peer(o * stride, mi),
            device_id_type=pl.DeviceIdType.MESH,
        )

    def reduce_start(source, target, x):
        each(1, owners, lambda off: reduce_copy(source, target, x, off).start())
        if stride > 1:
            pl.when(lax.rem(me, stride) != 0)(
                lambda: reduce_copy(source, target, x, 0).start()
            )

    def reduce_sent(source, target, x):
        each(1, owners, lambda off: reduce_copy(source, target, x, off).wait_send())
        if stride > 1:
            pl.when(lax.rem(me, stride) != 0)(
                lambda: reduce_copy(source, target, x, 0).wait_send()
            )

    def reduce_finish(source, target, x, result):
        result[...] = source[mine]

        def add(off):
            src = lax.rem(me + off, n)
            pltpu.make_async_remote_copy(
                src_ref=source.at[0],
                dst_ref=target.at[src],
                send_sem=rs_ss.at[x, 0],
                recv_sem=rs_rs.at[x, src],
                device_id=peer(src, mi),
                device_id_type=pl.DeviceIdType.MESH,
            ).wait_recv()
            result[...] += target[src]

        each(1, n, add)

    def gather_copy(block, x, off):
        red, mem = peer_of(off)
        return pltpu.make_async_remote_copy(
            src_ref=block,
            dst_ref=block,
            send_sem=ag_ss.at[x, off],
            recv_sem=ag_rs.at[x, mi * owners + mine],
            device_id=peer(red, mem),
            device_id_type=pl.DeviceIdType.MESH,
        )

    def gather_wait(ref, x, mem, o, red):
        pltpu.make_async_remote_copy(
            src_ref=ref,
            dst_ref=ref,
            send_sem=ag_ss.at[x, 0],
            recv_sem=ag_rs.at[x, mem * owners + o],
            device_id=peer(red, mem),
            device_id_type=pl.DeviceIdType.MESH,
        ).wait_recv()

    def gather_all(block_of, x, mems):
        def one(q):
            o = lax.rem(mine + lax.rem(q, owners), owners)
            mem = lax.rem(mi + lax.div(q, owners), n_mem)
            gather_wait(block_of(mem, o), x, mem, o, o * stride)

        each(1, mems * owners, one)
        if stride > 1:
            pl.when(lax.rem(me, stride) != 0)(lambda: one(0))

    for b in range(BATCHES):
        reduce_start(part.at[b], rs.at[b], b)
    for b in range(BATCHES):

        def finish(b=b):
            block = ag.at[b, mi, mine]
            reduce_finish(part.at[b], rs.at[b], b, block)
            each(1, total, lambda off: gather_copy(block, b, off).start())

        owner_only(finish)

    def slot(b, s):
        return ag[b, s].reshape(P_SIZE, own)

    def load_work(columns, b):
        cov = 0.0
        for s in range(n_mem):
            cov = cov + lax.dot_general(
                columns[s], columns[s], LAST, precision=HIGH, preferred_element_type=F32
            )
        r = lax.broadcasted_iota(jnp.int32, (P_SIZE, P_SIZE), 0)
        eye = r == lax.broadcasted_iota(jnp.int32, (P_SIZE, P_SIZE), 1)
        v = var_b[b * P_SIZE : (b + 1) * P_SIZE, :]
        work[:, :P_SIZE] = cov * (1.0 / (M - 1)) + jnp.where(eye, v, 0.0)
        work[:, P_SIZE : 2 * P_SIZE] = jnp.where(eye, 1.0, 0.0)
        for s in range(n_mem):
            lo = 2 * P_SIZE + s * own
            work[:, lo : lo + own] = columns[s]

    def taper(b, at):
        lo = b * P_SIZE
        row = lax.broadcasted_iota(jnp.int32, (P_SIZE, TILE), 1) + at
        c = jnp.concatenate([col_c[lo : lo + P_SIZE, :]] * (TILE // P_SIZE), axis=1)
        r = jnp.concatenate([col_r[lo : lo + P_SIZE, :]] * (TILE // P_SIZE), axis=1)
        near = jnp.maximum(1.0 - jnp.abs(row.astype(F32) - c) * r, 0.0)
        return near * near * (1.0 / (M - 1))

    gather_all(lambda mem, o: ag.at[0, mem, o], 0, n_mem)
    first = [slot(0, s) for s in range(n_mem)]
    load_work(first, 0)
    first_b = [x.astype(BF16) for x in first]

    def e_wait(off):
        src = lax.rem(mi + off, n_mem)
        pltpu.make_async_remote_copy(
            src_ref=state,
            dst_ref=e_all.at[src],
            send_sem=e_ss.at[0],
            recv_sem=e_rs.at[src],
            device_id=peer(me, src),
            device_id_type=pl.DeviceIdType.MESH,
        ).wait_recv()

    each(1, n_mem, e_wait)

    def cross_tile(t, carry):
        at = pl.multiple_of(t * TILE, TILE)
        cross = 0.0
        for s in range(n_mem):
            cross = cross + jnp.dot(
                first_b[s], e_all[s, :, pl.ds(at, TILE)], preferred_element_type=F32
            )
        tapered = (taper(0, at) * cross).astype(BF16)
        tap[:, pl.ds(at, TILE)] = tapered
        return carry

    lax.fori_loop(0, n_tiles, cross_tile, 0)
    change = lax.dot_general(
        foot[P_SIZE : 2 * P_SIZE, :], tap[...], LAST, preferred_element_type=F32
    )
    for o in range(owners):
        cpart[o] = change[o * chunk : (o + 1) * chunk, :]
    reduce_start(cpart, crs, BATCHES)

    sweep(work, inv, solved, root_b.at[pl.ds(0, P_SIZE)])

    def finish_change():
        block = cag.at[mine]
        reduce_finish(cpart, crs, BATCHES, block)
        each(1, n, lambda off: gather_copy(block, BATCHES, off).start())

    owner_only(finish_change)

    def weights():
        return lax.dot_general(
            solved[...], inv[...], FIRST, precision=HIGH, preferred_element_type=F32
        )

    wts[...] = weights().astype(BF16)

    gather_all(lambda mem, o: ag.at[1, mem, o], 1, n_mem)
    gather_all(lambda mem, o: cag.at[o], BATCHES, 1)
    c_full = cag[...].reshape(P_SIZE, P_SIZE)
    second = []
    for s in range(n_mem):
        moved = lax.dot_general(
            c_full,
            wts[s * own : (s + 1) * own, :].astype(F32),
            LAST,
            precision=HIGH,
            preferred_element_type=F32,
        )
        second.append(slot(1, s) - moved)
    load_work(second, 1)
    second_b = [x.astype(BF16) for x in second]

    def second_tile(t, carry):
        at = pl.multiple_of(t * TILE, TILE)
        before = tap[:, pl.ds(at, TILE)]
        cross = 0.0
        for s in range(n_mem):
            moved = jnp.dot(
                wts[s * own : (s + 1) * own, :], before, preferred_element_type=F32
            )
            now = (e_all[s, :, pl.ds(at, TILE)].astype(F32) - moved).astype(BF16)
            e_all[s, :, pl.ds(at, TILE)] = now
            cross = cross + jnp.dot(second_b[s], now, preferred_element_type=F32)
        tap[:, pl.ds(at, TILE)] = (taper(1, at) * cross).astype(BF16)
        return carry

    lax.fori_loop(0, n_tiles, second_tile, 0)
    sweep(work, inv, solved, root_b.at[pl.ds(P_SIZE, P_SIZE)])
    wts[...] = weights().astype(BF16)
    own_w = wts[pl.ds(pl.multiple_of(mi * own, own), own), :]

    def last_tile(t, carry):
        at = pl.multiple_of(t * TILE, TILE)
        moved = jnp.dot(own_w, tap[:, pl.ds(at, TILE)], preferred_element_type=F32)
        out[:, pl.ds(at, TILE)] = (
            e_all[mi, :, pl.ds(at, TILE)].astype(F32) - moved
        ).astype(BF16)
        return carry

    lax.fori_loop(0, n_tiles, last_tile, 0)

    each(1, n_mem, lambda off: e_copy(off).wait_send())
    for b in range(BATCHES):
        reduce_sent(part.at[b], rs.at[b], b)

        def sent(b=b):
            each(1, total, lambda off: gather_copy(ag.at[b, mi, mine], b, off).wait_send())

        owner_only(sent)
    reduce_sent(cpart, crs, BATCHES)

    def change_sent():
        each(1, n, lambda off: gather_copy(cag.at[mine], BATCHES, off).wait_send())

    owner_only(change_sent)


def on_device(shape, state, centers, half_width, radius, order, obs_var):
    n_slab, n_mem, n_sub = shape
    own, rows = state.shape
    n = n_slab * n_sub
    total = n * n_mem
    owners = min(n, 8)
    chunk = P_SIZE // owners
    n_obs = BATCHES * P_SIZE
    vmem = pl.BlockSpec(memory_space=pltpu.VMEM)
    return pl.pallas_call(
        functools.partial(kernel, shape),
        out_shape=jax.ShapeDtypeStruct((own, rows), BF16),
        in_specs=[vmem] * 6,
        out_specs=vmem,
        scratch_shapes=[
            pltpu.VMEM((n_mem, own, rows), BF16),
            pltpu.VMEM((n_obs, rows), BF16),
            pltpu.VMEM((P_SIZE, rows), BF16),
            pltpu.VMEM((n_obs, P_SIZE), F32),
            pltpu.VMEM((n_obs, P_SIZE), F32),
            pltpu.VMEM((n_obs, P_SIZE), F32),
            pltpu.VMEM((n_obs, P_SIZE), F32),
            pltpu.VMEM((P_SIZE, 2 * P_SIZE + M), F32),
            pltpu.VMEM((P_SIZE, P_SIZE), F32),
            pltpu.VMEM((P_SIZE, M), F32),
            pltpu.VMEM((M, P_SIZE), BF16),
            pltpu.VMEM((BATCHES, owners, chunk, own), F32),
            pltpu.VMEM((BATCHES, n, chunk, own), F32),
            pltpu.VMEM((BATCHES, n_mem, owners, chunk, own), F32),
            pltpu.VMEM((owners, chunk, P_SIZE), F32),
            pltpu.VMEM((n, chunk, P_SIZE), F32),
            pltpu.VMEM((owners, chunk, P_SIZE), F32),
            pltpu.SemaphoreType.DMA((n_mem,)),
            pltpu.SemaphoreType.DMA((n_mem,)),
            pltpu.SemaphoreType.DMA((BATCHES + 1, owners)),
            pltpu.SemaphoreType.DMA((BATCHES + 1, n)),
            pltpu.SemaphoreType.DMA((BATCHES + 1, total)),
            pltpu.SemaphoreType.DMA((BATCHES + 1, n_mem * owners)),
        ],
        compiler_params=pltpu.CompilerParams(
            collective_id=0, has_side_effects=True, vmem_limit_bytes=40 * 1024 * 1024
        ),
    )(
        state,
        centers[None, :],
        half_width[None, :],
        radius[None, :],
        order[None, :],
        obs_var[None, :],
    )


def solution(mesh):
    shape = (mesh.shape["slab"], mesh.shape["mem"], mesh.shape["sub"])
    placed = (P("mem", ("grp", "slab", "sub")), P("grp"), P("grp"), P("grp"), P("grp"), P("grp"))
    return jax.shard_map(
        functools.partial(on_device, shape),
        mesh=mesh,
        in_specs=placed,
        out_specs=P("mem", ("grp", "slab", "sub")),
        check_vma=False,
    )
```

time: 216 us -> 45.3 us (0.21)
  waiting for transfers between devices: 104 us -> 0 us
  other arithmetic: 65.5 us -> 0 us
  Pallas kernels: 0 us -> 42.5 us
  between operations: 15.2 us -> 0.02 us
  blocking collectives: 10.7 us -> 0 us
  matrix products: 9.54 us -> 0 us
  local copies, waits for them, and re-layouts: 10.8 us -> 2.57 us
    psum x2 -> x0, waiting for transfers between devices: 103 us -> none  [on_device(): summed_own = lax.psum(partial_value, ('slab', 'sub'))]
    another operation x12 -> x0, other arithmetic: 65.5 us -> none  [the longest x6 24.8 us: gain_terms(): factor = jnp.linalg.cholesky(covariance)]
    pallas_call x0 -> x1, Pallas kernels: none -> 42.5 us  [on_device(): pl.pallas_call(functools.partial(kernel, shape), out_shape=jax.ShapeDtype...]
    all_gather x2 -> x0, blocking collectives: 10.7 us -> none  [on_device(): projected = lax.all_gather(summed_own, 'mem', axis=0, tiled=True)]
    dot_general x8 -> x0, matrix products: 8.56 us -> none  [the longest x2 4.76 us: on_device(): jnp.dot(weights_own, tapered, preferred_element_type=jnp.float32)]
    gather x4 -> x0, local copies, waits for them, and re-layouts: 7.79 us -> none  [the longest x1 1.95 us: on_device(): half_all = half_width[order]]
  transfers between devices with their start and end apart: 4 -> 0, of which waited for: 2 -> 0; matrix products, arithmetic and copies ran while one was open for 33% -> 0% of each run, Pallas kernels for 0% -> 0%
where the time goes in v1:
time: 45.3 us; the launch traced here: 45.1 us
  Pallas kernels  42.5 us (94%)
  local copies, waits for them, and re-layouts  2.57 us (6%)
    pallas_call x1, Pallas kernels, on_device(): pl.pallas_call(functools.partial(kernel, shape), out_shape=jax.ShapeDtype...  42.5 us
    unnamed x13, local copies, waits for them, and re-layouts  2.57 us

profile of v1, /device:TPU:0, one launch (start us, length us, event | category | flops | bytes accessed | tf_op | source)
XLA Modules:
  0.0 45.1 jit_solution(4897938515792178039)
XLA Ops:
  0.0 0.0 copy-start.4
  0.0 0.0 copy-start.5
  0.0 0.0 copy-start.2
  0.0 0.0 copy-start.3
  0.0 0.0 copy-start.1
  0.0 0.7 %copy-done.4 = s32[256]{0:T(256)S(1)} copy-done((s32[256]{0:T(256)S(1)}, s32[256]{0:T(256)}, u32[]{:S(2)}) %copy-start.4) | copy-done | bytes 1048
  0.7 0.0 copy-done.5
  0.7 0.0 copy-done.2
  0.7 0.0 copy-done.3
  0.7 0.0 copy-done.1
  0.7 0.0 copy-start
  0.7 1.0 %copy-done = bf16[128,2048]{1,0:T(8,128)(2,1)S(1)} copy-done((bf16[128,2048]{1,0:T(8,128)(2,1)S(1)}, bf16[128,2048]{1,0:T(8,128)(2,1)}, u32[]{:S(2)}) %copy-start) | copy-done | bytes 524312
  1.8 42.5 %shard_map.64 = bf16[128,2048]{1,0:T(8,128)(2,1)S(1)} custom-call(bf16[128,2048]{1,0:T(8,128)(2,1)S(1)} %copy-done, s32[1,256]{1,0:T(1,128)S(1)} %bitcast.5, s32[1,256]{1,0:T(1,128)S(1)} %bitcast.6, s32[1,256]{1,0:T(1,128)S(1)} %bitcast.7, s32[1,256]{1,0:T(1,128)S(1)} %bitcast.8, f32[1,256]{1,0:T(1,128)S(1)} %bitcast.9), custom_call_target="tpu_custom_call" | custom-call | tf_op jit(solution)/shard_map/pallas_call | solution.py:412
  44.3 0.8 %copy.8 = bf16[128,2048]{1,0:T(8,128)(2,1)} copy(bf16[128,2048]{1,0:T(8,128)(2,1)S(1)} %shard_map.64) | data formatting | bytes 1048576
Async XLA Ops:
  0.0 0.7 %copy-start.4 = (s32[256]{0:T(256)S(1)}, s32[256]{0:T(256)}, u32[]{:S(2)}) copy-start(s32[256]{0:T(256)} %param.10) | copy-start | bytes 3076
  0.0 0.7 %copy-start.5 = (f32[256]{0:T(256)S(1)}, f32[256]{0:T(256)}, u32[]{:S(2)}) copy-start(f32[256]{0:T(256)} %param.11) | copy-start | bytes 3076
  0.0 0.7 %copy-start.2 = (s32[256]{0:T(256)S(1)}, s32[256]{0:T(256)}, u32[]{:S(2)}) copy-start(s32[256]{0:T(256)} %param.8) | copy-start | bytes 3076
  0.0 0.7 %copy-start.3 = (s32[256]{0:T(256)S(1)}, s32[256]{0:T(256)}, u32[]{:S(2)}) copy-start(s32[256]{0:T(256)} %param.9) | copy-start | bytes 3076
  0.0 0.7 %copy-start.1 = (s32[256]{0:T(256)S(1)}, s32[256]{0:T(256)}, u32[]{:S(2)}) copy-start(s32[256]{0:T(256)} %param.7) | copy-start | bytes 3076
  0.7 1.0 %copy-start = (bf16[128,2048]{1,0:T(8,128)(2,1)S(1)}, bf16[128,2048]{1,0:T(8,128)(2,1)}, u32[]{:S(2)}) copy-start(bf16[128,2048]{1,0:T(8,128)(2,1)} %state.1) | copy-start | bytes 1572868

commit v2 on v1

v2 whole, which is shorter than its diff:
```python
import functools
import math

import jax
import jax.numpy as jnp
from jax import lax
from jax.experimental import pallas as pl
from jax.experimental.pallas import tpu as pltpu
from jax.sharding import PartitionSpec as P

M = 256
P_SIZE = 128
BATCHES = 2
BLOCK = 16

FLOOR = math.exp(-2.0)
F32 = jnp.float32
BF16 = jnp.bfloat16
HIGH = lax.Precision.HIGHEST
LAST = (((1,), (1,)), ((), ()))
FIRST = (((0,), (0,)), ((), ()))


def each(start, stop, body):
    if stop - start <= 16:
        for i in range(start, stop):
            body(i)
    else:

        def step(i, carry):
            body(i)
            return carry

        lax.fori_loop(start, stop, step, 0)


def split3(x):
    high = x.astype(BF16)
    rest = x - high.astype(F32)
    mid = rest.astype(BF16)
    low = (rest - mid.astype(F32)).astype(BF16)
    return high, mid, low


def sweep(work, inv, solved, root):
    b = BLOCK
    width = work.shape[1] // P_SIZE

    def step(k, carry):
        r0 = pl.multiple_of(k * b, b)
        parts = [work[pl.ds(r0, b), g * P_SIZE : (g + 1) * P_SIZE] for g in range(width)]
        roots = root[pl.ds(r0, b), :]
        rolled = pltpu.roll(parts[0], lax.rem(P_SIZE - r0, P_SIZE), 1)
        cols = [jnp.broadcast_to(rolled[:, j : j + 1], (b, P_SIZE)) for j in range(b)]
        row_id = lax.broadcasted_iota(jnp.int32, (b, P_SIZE), 0)
        for j in range(b):
            pivot = cols[j][j : j + 1, :]
            scale = lax.rsqrt(pivot)
            scale_m = 1.0 / (pivot * scale + roots[j : j + 1, :])
            column = jnp.where(row_id > j, cols[j] * scale, 0.0)
            for i in range(j + 1, b):
                cols[i] = cols[i] - column * column[i : i + 1, :]
            for g in range(width):
                row = parts[g][j : j + 1, :] * (scale if g < 2 else scale_m)
                parts[g] = jnp.where(row_id == j, row, parts[g] - column * row)
        inv[pl.ds(r0, b), :] = parts[1]
        for g in range(2, width):
            solved[pl.ds(r0, b), (g - 2) * P_SIZE : (g - 1) * P_SIZE] = parts[g]
        pieces = [split3(x) for x in parts]
        h, m, l = pieces[0]
        left = jnp.concatenate([h, h, m, h, m, l], axis=0)
        h, m, l = (jnp.concatenate([x[n] for x in pieces], axis=1) for n in range(3))
        right = jnp.concatenate([h, m, h, l, m, h], axis=0)
        work[...] -= lax.dot_general(left, right, FIRST, preferred_element_type=F32)
        return carry

    lax.fori_loop(0, P_SIZE // b, step, 0)


def kernel(
    shape,
    state_hbm, cen_hbm, half_hbm, rad_hbm, order_hbm, var_hbm,
    out,
    state, cen, half, rad, order, var,
    e_all, foot, tap, tap1, col_c, col_r, var_b, root_b, work, inv, solved, wts,
    part, rs, ag, cpart, crs, cag,
    in_s, e_ss, e_rs, t_ss, t_rs, rs_ss, rs_rs, crs_ss, crs_rs, ag_ss, ag_rs, cag_ss, cag_rs,
):
    n_slab, n_mem, n_sub = shape
    n = n_slab * n_sub
    total = n * n_mem
    own, rows = state.shape
    part_rows = rows // n_mem

    mi = lax.axis_index("mem")
    me = lax.axis_index("slab") * n_sub + lax.axis_index("sub")

    def peer(red, mem):
        return {"slab": lax.div(red, n_sub), "sub": lax.rem(red, n_sub), "mem": mem}

    def peer_of(off):
        red = lax.rem(me + lax.rem(off, n), n)
        mem = lax.rem(mi + lax.div(off, n), n_mem)
        return red, mem

    inputs = [
        pltpu.make_async_copy(a, b, in_s.at[i])
        for i, (a, b) in enumerate(
            zip(
                (state_hbm, cen_hbm, half_hbm, rad_hbm, order_hbm, var_hbm),
                (state, cen, half, rad, order, var),
            )
        )
    ]
    for copy in inputs[1:] + inputs[:1]:
        copy.start()

    barrier = pltpu.get_barrier_semaphore()

    def greet(off):
        red, mem = peer_of(off)
        pl.semaphore_signal(
            barrier, inc=1, device_id=peer(red, mem), device_id_type=pl.DeviceIdType.MESH
        )

    each(1, total, greet)
    for copy in inputs[1:]:
        copy.wait()

    n_obs = BATCHES * P_SIZE
    picked = jnp.broadcast_to(order[...].astype(F32), (P_SIZE, n_obs)).T.astype(jnp.int32)
    lane = lax.broadcasted_iota(jnp.int32, (n_obs, P_SIZE), 1)
    masks = [picked == lane + h * P_SIZE for h in range(BATCHES)]

    def pick(ref):
        value = ref[...].astype(F32)
        chosen = 0.0
        for h in range(BATCHES):
            chosen = chosen + jnp.where(masks[h], value[:, h * P_SIZE : (h + 1) * P_SIZE], 0.0)
        return jnp.sum(chosen, axis=1, keepdims=True)

    center = pick(cen) - (me * rows).astype(F32)
    width = pick(half)
    variance = pick(var)
    col_c[...] = jnp.broadcast_to(center, (n_obs, P_SIZE))
    col_r[...] = jnp.broadcast_to(1.0 / pick(rad), (n_obs, P_SIZE))
    var_b[...] = jnp.broadcast_to(variance, (n_obs, P_SIZE))
    root_b[...] = jnp.broadcast_to(jnp.sqrt(variance), (n_obs, P_SIZE))
    steep = -2.0 / (width * width)
    height = 1.0 / jnp.sqrt(width)

    pl.semaphore_wait(barrier, total - 1)

    def rows_of(mem):
        return pl.ds(pl.multiple_of(mem * part_rows, part_rows), part_rows)

    my_rows = rows_of(mi)

    def e_copy(off):
        to = lax.rem(mi + off, n_mem)
        return pltpu.make_async_remote_copy(
            src_ref=state_hbm.at[:, rows_of(to)],
            dst_ref=e_all.at[mi],
            send_sem=e_ss.at[off],
            recv_sem=e_rs.at[mi],
            device_id=peer(me, to),
            device_id_type=pl.DeviceIdType.MESH,
        )

    each(1, n_mem, lambda off: e_copy(off).start())

    def foot_tile(t, carry):
        at = pl.multiple_of(t * 256, 256)
        row = lax.broadcasted_iota(jnp.int32, (n_obs, 256), 1) + at
        distance = row.astype(F32) - center
        shape_f = jnp.maximum(jnp.exp(distance * distance * steep) - FLOOR, 0.0) * height
        foot[:, pl.ds(at, 256)] = shape_f.astype(BF16)
        return carry

    lax.fori_loop(0, rows // 256, foot_tile, 0)
    inputs[0].wait()
    e_all[mi] = state[:, my_rows]
    sums = lax.dot_general(foot[...], state[...], LAST, preferred_element_type=F32)
    for b in range(BATCHES):
        part[b] = sums[b * P_SIZE : (b + 1) * P_SIZE, :].reshape(part.shape[1:])

    class Sum:
        def __init__(self, size, index, device, source, target, result, everyone, sems):
            self.size, self.index, self.device = size, index, device
            self.source, self.target, self.result, self.everyone = source, target, result, everyone
            self.rs_ss, self.rs_rs, self.ag_ss, self.ag_rs = sems
            self.owners = source.shape[0]
            self.stride = size // self.owners
            self.mine = lax.div(index, self.stride)

        def remote(self, src, dst, send, recv, device):
            return pltpu.make_async_remote_copy(
                src_ref=src, dst_ref=dst, send_sem=send, recv_sem=recv,
                device_id=device, device_id_type=pl.DeviceIdType.MESH,
            )

        def if_owner(self, body, owner=True):
            if self.stride == 1:
                if owner:
                    body()
            else:
                pl.when((lax.rem(self.index, self.stride) == 0) == owner)(body)

        def out_copy(self, off):
            o = lax.rem(self.mine + off, self.owners)
            return self.remote(
                self.source.at[o], self.target.at[self.index],
                self.rs_ss.at[off], self.rs_rs.at[self.index], self.device(o * self.stride),
            )

        def start(self):
            each(1, self.owners, lambda off: self.out_copy(off).start())
            self.if_owner(lambda: self.out_copy(0).start(), False)

        def gather_copy(self, off):
            block = self.result(mi, self.mine)
            return self.remote(
                block, block, self.ag_ss.at[off],
                self.ag_rs.at[mi if self.everyone else 0, self.mine], peer(*peer_of(off)),
            )

        def finish(self):
            def body():
                for off in range(1, self.size) if self.size <= 16 else ():
                    self.arrived(lax.rem(self.index + off, self.size))
                block = self.result(mi, self.mine)
                value = self.source[self.mine]
                if self.size <= 16:
                    for off in range(1, self.size):
                        value = value + self.target[lax.rem(self.index + off, self.size)]
                    block[...] = value
                else:
                    block[...] = value

                    def add(off):
                        src = lax.rem(self.index + off, self.size)
                        self.arrived(src)
                        block[...] += self.target[src]

                    each(1, self.size, add)
                each(1, total, lambda off: self.gather_copy(off).start())

            self.if_owner(body)

        def arrived(self, src):
            self.remote(
                self.source.at[0], self.target.at[src], self.rs_ss.at[0], self.rs_rs.at[src],
                self.device(src),
            ).wait_recv()

        def gather(self):
            mems = n_mem if self.everyone else 1

            def one(q):
                o = lax.rem(self.mine + lax.rem(q, self.owners), self.owners)
                mem = lax.rem(mi + lax.div(q, self.owners), n_mem)
                block = self.result(mem, o)
                self.remote(
                    block, block, self.ag_ss.at[0],
                    self.ag_rs.at[mem if self.everyone else 0, o],
                    self.device(o * self.stride),
                ).wait_recv()

            each(1, mems * self.owners, one)
            self.if_owner(lambda: one(0), False)

        def sent(self):
            each(1, self.owners, lambda off: self.out_copy(off).wait_send())
            self.if_owner(lambda: self.out_copy(0).wait_send(), False)
            self.if_owner(
                lambda: each(1, total, lambda off: self.gather_copy(off).wait_send())
            )

    projections = [
        Sum(
            n, me, lambda i: peer(i, mi), part.at[b], rs.at[b],
            lambda mem, o, b=b: ag.at[b, mem, o], True,
            (rs_ss.at[b], rs_rs.at[b], ag_ss.at[b], ag_rs.at[b]),
        )
        for b in range(BATCHES)
    ]
    changes = Sum(
        total, mi * n + me, lambda i: peer(lax.rem(i, n), lax.div(i, n)), cpart, crs,
        lambda mem, o: cag.at[o], False, (crs_ss, crs_rs, cag_ss, cag_rs),
    )
    for x in projections:
        x.start()
    for x in projections:
        x.finish()

    def slot(b, s):
        return ag[b, s].reshape(P_SIZE, own)

    def load_work(columns, b):
        cov = 0.0
        for s in range(n_mem):
            cov = cov + lax.dot_general(
                columns[s], columns[s], LAST, precision=HIGH, preferred_element_type=F32
            )
        r = lax.broadcasted_iota(jnp.int32, (P_SIZE, P_SIZE), 0)
        eye = r == lax.broadcasted_iota(jnp.int32, (P_SIZE, P_SIZE), 1)
        v = var_b[b * P_SIZE : (b + 1) * P_SIZE, :]
        work[:, :P_SIZE] = cov * (1.0 / (M - 1)) + jnp.where(eye, v, 0.0)
        work[:, P_SIZE : 2 * P_SIZE] = jnp.where(eye, 1.0, 0.0)
        for s in range(n_mem):
            lo = 2 * P_SIZE + s * own
            work[:, lo : lo + own] = columns[s]

    def taper(b):
        lo = b * P_SIZE
        row = lax.broadcasted_iota(jnp.int32, (P_SIZE, part_rows), 1) + mi * part_rows
        c = jnp.concatenate([col_c[lo : lo + P_SIZE, :]] * (part_rows // P_SIZE), axis=1)
        r = jnp.concatenate([col_r[lo : lo + P_SIZE, :]] * (part_rows // P_SIZE), axis=1)
        near = jnp.maximum(1.0 - jnp.abs(row.astype(F32) - c) * r, 0.0)
        return near * near * (1.0 / (M - 1))

    def t_copy(x, ref, off):
        return pltpu.make_async_remote_copy(
            src_ref=ref.at[mi],
            dst_ref=ref.at[mi],
            send_sem=t_ss.at[x, off],
            recv_sem=t_rs.at[x, mi],
            device_id=peer(me, lax.rem(mi + off, n_mem)),
            device_id_type=pl.DeviceIdType.MESH,
        )

    def t_wait(x, ref, off):
        src = lax.rem(mi + off, n_mem)
        pltpu.make_async_remote_copy(
            src_ref=ref.at[src],
            dst_ref=ref.at[src],
            send_sem=t_ss.at[x, 0],
            recv_sem=t_rs.at[x, src],
            device_id=peer(me, src),
            device_id_type=pl.DeviceIdType.MESH,
        ).wait_recv()

    projections[0].gather()
    first = [slot(0, s) for s in range(n_mem)]
    first_b = [x.astype(BF16) for x in first]

    def e_wait(off):
        src = lax.rem(mi + off, n_mem)
        pltpu.make_async_remote_copy(
            src_ref=e_all.at[src],
            dst_ref=e_all.at[src],
            send_sem=e_ss.at[0],
            recv_sem=e_rs.at[src],
            device_id=peer(me, src),
            device_id_type=pl.DeviceIdType.MESH,
        ).wait_recv()

    each(1, n_mem, e_wait)

    cross = 0.0
    for s in range(n_mem):
        cross = cross + jnp.dot(first_b[s], e_all[s], preferred_element_type=F32)
    before = (taper(0) * cross).astype(BF16)
    tap[mi] = before
    change = lax.dot_general(
        foot[P_SIZE : 2 * P_SIZE, my_rows], before, LAST, preferred_element_type=F32
    )
    cpart[...] = change.reshape(cpart.shape)
    changes.start()
    each(1, n_mem, lambda off: t_copy(0, tap, off).start())

    load_work(first, 0)
    sweep(work, inv, solved, root_b.at[pl.ds(0, P_SIZE)])
    changes.finish()

    def weights():
        return lax.dot_general(
            solved[...], inv[...], FIRST, precision=HIGH, preferred_element_type=F32
        )

    wts[...] = weights().astype(BF16)

    projections[1].gather()
    changes.gather()
    c_full = cag[...].reshape(P_SIZE, P_SIZE)
    second = []
    for s in range(n_mem):
        moved = lax.dot_general(
            c_full,
            wts[s * own : (s + 1) * own, :].astype(F32),
            LAST,
            precision=HIGH,
            preferred_element_type=F32,
        )
        second.append(slot(1, s) - moved)
    second_b = [x.astype(BF16) for x in second]

    before = tap[mi]
    cross = 0.0
    for s in range(n_mem):
        moved = jnp.dot(wts[s * own : (s + 1) * own, :], before, preferred_element_type=F32)
        now = (e_all[s].astype(F32) - moved).astype(BF16)
        cross = cross + jnp.dot(second_b[s], now, preferred_element_type=F32)
    tap1[mi] = (taper(1) * cross).astype(BF16)
    each(1, n_mem, lambda off: t_copy(1, tap1, off).start())

    load_work(second, 1)
    own_w = wts[pl.ds(pl.multiple_of(mi * own, own), own), :]
    each(1, n_mem, lambda off: t_wait(0, tap, off))
    for mem in range(n_mem):
        at = slice(mem * part_rows, (mem + 1) * part_rows)
        moved = jnp.dot(own_w, tap[mem], preferred_element_type=F32)
        out[:, at] = (state[:, at].astype(F32) - moved).astype(BF16)

    sweep(work, inv, solved, root_b.at[pl.ds(P_SIZE, P_SIZE)])
    wts[...] = weights().astype(BF16)
    own_w = wts[pl.ds(pl.multiple_of(mi * own, own), own), :]

    each(1, n_mem, lambda off: t_wait(1, tap1, off))
    for mem in range(n_mem):
        at = slice(mem * part_rows, (mem + 1) * part_rows)
        moved = jnp.dot(own_w, tap1[mem], preferred_element_type=F32)
        out[:, at] = (out[:, at].astype(F32) - moved).astype(BF16)

    each(1, n_mem, lambda off: e_copy(off).wait_send())
    for x, ref in enumerate((tap, tap1)):
        each(1, n_mem, lambda off: t_copy(x, ref, off).wait_send())
    for x in projections + [changes]:
        x.sent()


def on_device(shape, state, centers, half_width, radius, order, obs_var):
    n_slab, n_mem, n_sub = shape
    own, rows = state.shape
    n = n_slab * n_sub
    total = n * n_mem
    owners = min(n, 8)
    chunk = P_SIZE // owners
    c_owners = min(total, 16)
    c_chunk = P_SIZE // c_owners
    n_obs = BATCHES * P_SIZE
    part_rows = rows // n_mem
    hbm = pl.BlockSpec(memory_space=pltpu.HBM)
    vmem = pl.BlockSpec(memory_space=pltpu.VMEM)
    return pl.pallas_call(
        functools.partial(kernel, shape),
        out_shape=jax.ShapeDtypeStruct((own, rows), BF16),
        in_specs=[hbm] * 6,
        out_specs=vmem,
        scratch_shapes=[
            pltpu.VMEM((own, rows), BF16),
            pltpu.VMEM((1, n_obs), jnp.int32),
            pltpu.VMEM((1, n_obs), jnp.int32),
            pltpu.VMEM((1, n_obs), jnp.int32),
            pltpu.VMEM((1, n_obs), jnp.int32),
            pltpu.VMEM((1, n_obs), F32),
            pltpu.VMEM((n_mem, own, part_rows), BF16),
            pltpu.VMEM((n_obs, rows), BF16),
            pltpu.VMEM((n_mem, P_SIZE, part_rows), BF16),
            pltpu.VMEM((n_mem, P_SIZE, part_rows), BF16),
            pltpu.VMEM((n_obs, P_SIZE), F32),
            pltpu.VMEM((n_obs, P_SIZE), F32),
            pltpu.VMEM((n_obs, P_SIZE), F32),
            pltpu.VMEM((n_obs, P_SIZE), F32),
            pltpu.VMEM((P_SIZE, 2 * P_SIZE + M), F32),
            pltpu.VMEM((P_SIZE, P_SIZE), F32),
            pltpu.VMEM((P_SIZE, M), F32),
            pltpu.VMEM((M, P_SIZE), BF16),
            pltpu.VMEM((BATCHES, owners, chunk, own), F32),
            pltpu.VMEM((BATCHES, n, chunk, own), F32),
            pltpu.VMEM((BATCHES, n_mem, owners, chunk, own), F32),
            pltpu.VMEM((c_owners, c_chunk, P_SIZE), F32),
            pltpu.VMEM((total, c_chunk, P_SIZE), F32),
            pltpu.VMEM((c_owners, c_chunk, P_SIZE), F32),
            pltpu.SemaphoreType.DMA((6,)),
            pltpu.SemaphoreType.DMA((n_mem,)),
            pltpu.SemaphoreType.DMA((n_mem,)),
            pltpu.SemaphoreType.DMA((BATCHES, n_mem)),
            pltpu.SemaphoreType.DMA((BATCHES, n_mem)),
            pltpu.SemaphoreType.DMA((BATCHES, owners)),
            pltpu.SemaphoreType.DMA((BATCHES, n)),
            pltpu.SemaphoreType.DMA((c_owners,)),
            pltpu.SemaphoreType.DMA((total,)),
            pltpu.SemaphoreType.DMA((BATCHES, total)),
            pltpu.SemaphoreType.DMA((BATCHES, n_mem, owners)),
            pltpu.SemaphoreType.DMA((total,)),
            pltpu.SemaphoreType.DMA((1, c_owners)),
        ],
        compiler_params=pltpu.CompilerParams(
            collective_id=0, has_side_effects=True, vmem_limit_bytes=40 * 1024 * 1024
        ),
    )(
        state,
        centers[None, :],
        half_width[None, :],
        radius[None, :],
        order[None, :],
        obs_var[None, :],
    )


def solution(mesh):
    shape = (mesh.shape["slab"], mesh.shape["mem"], mesh.shape["sub"])
    placed = (P("mem", ("grp", "slab", "sub")), P("grp"), P("grp"), P("grp"), P("grp"), P("grp"))
    return jax.shard_map(
        functools.partial(on_device, shape),
        mesh=mesh,
        in_specs=placed,
        out_specs=P("mem", ("grp", "slab", "sub")),
        check_vma=False,
    )
```

time: 45.3 us -> 40.4 us (0.89)
  Pallas kernels: 42.5 us -> 37.6 us
    pallas_call x1, Pallas kernels: 42.5 us -> 37.6 us  [on_device(): pl.pallas_call(functools.partial(kernel, shape), out_shape=jax.ShapeDtype...]
where the time goes in v2:
time: 40.4 us; the launch traced here: 40.2 us
  Pallas kernels  37.6 us (93%)
  local copies, waits for them, and re-layouts  2.57 us (6%)
    pallas_call x1, Pallas kernels, on_device(): pl.pallas_call(functools.partial(kernel, shape), out_shape=jax.ShapeDtype...  37.6 us
    unnamed x13, local copies, waits for them, and re-layouts  2.57 us

profile of v2, /device:TPU:0, one launch (start us, length us, event | category | flops | bytes accessed | tf_op | source)
XLA Modules:
  0.0 40.2 jit_solution(14785989950211111309)
XLA Ops:
  0.0 0.0 copy-start.4
  0.0 0.0 copy-start.5
  0.0 0.0 copy-start.2
  0.0 0.0 copy-start.3
  0.0 0.0 copy-start.1
  0.0 0.7 %copy-done.4 = s32[256]{0:T(256)S(1)} copy-done((s32[256]{0:T(256)S(1)}, s32[256]{0:T(256)}, u32[]{:S(2)}) %copy-start.4) | copy-done | bytes 1048
  0.7 0.0 copy-done.5
  0.7 0.0 copy-done.2
  0.7 0.0 copy-done.3
  0.7 0.0 copy-done.1
  0.7 0.0 copy-start
  0.7 1.0 %copy-done = bf16[128,2048]{1,0:T(8,128)(2,1)S(1)} copy-done((bf16[128,2048]{1,0:T(8,128)(2,1)S(1)}, bf16[128,2048]{1,0:T(8,128)(2,1)}, u32[]{:S(2)}) %copy-start) | copy-done | bytes 524312
  1.8 37.6 %shard_map.64 = bf16[128,2048]{1,0:T(8,128)(2,1)S(1)} custom-call(bf16[128,2048]{1,0:T(8,128)(2,1)S(1)} %copy-done, s32[1,256]{1,0:T(1,128)S(1)} %bitcast.5, s32[1,256]{1,0:T(1,128)S(1)} %bitcast.6, s32[1,256]{1,0:T(1,128)S(1)} %bitcast.7, s32[1,256]{1,0:T(1,128)S(1)} %bitcast.8, f32[1,256]{1,0:T(1,128)S(1)} %bitcast.9), custom_call_target="tpu_custom_call" | custom-call | tf_op jit(solution)/shard_map/pallas_call | solution.py:445
  39.4 0.8 %copy.8 = bf16[128,2048]{1,0:T(8,128)(2,1)} copy(bf16[128,2048]{1,0:T(8,128)(2,1)S(1)} %shard_map.64) | data formatting | bytes 1048576
Async XLA Ops:
  0.0 0.7 %copy-start.4 = (s32[256]{0:T(256)S(1)}, s32[256]{0:T(256)}, u32[]{:S(2)}) copy-start(s32[256]{0:T(256)} %param.10) | copy-start | bytes 3076
  0.0 0.7 %copy-start.5 = (f32[256]{0:T(256)S(1)}, f32[256]{0:T(256)}, u32[]{:S(2)}) copy-start(f32[256]{0:T(256)} %param.11) | copy-start | bytes 3076
  0.0 0.7 %copy-start.2 = (s32[256]{0:T(256)S(1)}, s32[256]{0:T(256)}, u32[]{:S(2)}) copy-start(s32[256]{0:T(256)} %param.8) | copy-start | bytes 3076
  0.0 0.7 %copy-start.3 = (s32[256]{0:T(256)S(1)}, s32[256]{0:T(256)}, u32[]{:S(2)}) copy-start(s32[256]{0:T(256)} %param.9) | copy-start | bytes 3076
  0.0 0.7 %copy-start.1 = (s32[256]{0:T(256)S(1)}, s32[256]{0:T(256)}, u32[]{:S(2)}) copy-start(s32[256]{0:T(256)} %param.7) | copy-start | bytes 3076
  0.7 1.0 %copy-start = (bf16[128,2048]{1,0:T(8,128)(2,1)S(1)}, bf16[128,2048]{1,0:T(8,128)(2,1)}, u32[]{:S(2)}) copy-start(bf16[128,2048]{1,0:T(8,128)(2,1)} %state_hbm.1) | copy-start | bytes 1572868

commit v3 on v2

--- a/solution.py
+++ b/solution.py
@@ -12,6 +12,8 @@
 P_SIZE = 128
 BATCHES = 2
 BLOCK = 16
+SPLIT = 4
+SPLIT_2 = 4
 
 FLOOR = math.exp(-2.0)
 F32 = jnp.float32
@@ -42,7 +44,7 @@
     return high, mid, low
 
 
-def sweep(work, inv, solved, root):
+def sweep(work, inv, solved, root, first=0, last=P_SIZE // BLOCK):
     b = BLOCK
     width = work.shape[1] // P_SIZE
 
@@ -74,7 +76,7 @@
         work[...] -= lax.dot_general(left, right, FIRST, preferred_element_type=F32)
         return carry
 
-    lax.fori_loop(0, P_SIZE // b, step, 0)
+    lax.fori_loop(first, last, step, 0)
 
 
 def kernel(
@@ -149,8 +151,6 @@
     steep = -2.0 / (width * width)
     height = 1.0 / jnp.sqrt(width)
 
-    pl.semaphore_wait(barrier, total - 1)
-
     def rows_of(mem):
         return pl.ds(pl.multiple_of(mem * part_rows, part_rows), part_rows)
 
@@ -167,8 +167,6 @@
             device_id_type=pl.DeviceIdType.MESH,
         )
 
-    each(1, n_mem, lambda off: e_copy(off).start())
-
     def foot_tile(t, carry):
         at = pl.multiple_of(t * 256, 256)
         row = lax.broadcasted_iota(jnp.int32, (n_obs, 256), 1) + at
@@ -179,7 +177,6 @@
 
     lax.fori_loop(0, rows // 256, foot_tile, 0)
     inputs[0].wait()
-    e_all[mi] = state[:, my_rows]
     sums = lax.dot_general(foot[...], state[...], LAST, preferred_element_type=F32)
     for b in range(BATCHES):
         part[b] = sums[b * P_SIZE : (b + 1) * P_SIZE, :].reshape(part.shape[1:])
@@ -288,10 +285,12 @@
         total, mi * n + me, lambda i: peer(lax.rem(i, n), lax.div(i, n)), cpart, crs,
         lambda mem, o: cag.at[o], False, (crs_ss, crs_rs, cag_ss, cag_rs),
     )
+    pl.semaphore_wait(barrier, total - 1)
     for x in projections:
         x.start()
-    for x in projections:
-        x.finish()
+    each(1, n_mem, lambda off: e_copy(off).start())
+    e_all[mi] = state[:, my_rows]
+    projections[0].finish()
 
     def slot(b, s):
         return ag[b, s].reshape(P_SIZE, own)
@@ -367,11 +366,13 @@
     )
     cpart[...] = change.reshape(cpart.shape)
     changes.start()
+    projections[1].finish()
+
+    load_work(first, 0)
+    sweep(work, inv, solved, root_b.at[pl.ds(0, P_SIZE)], 0, SPLIT)
+    changes.finish()
     each(1, n_mem, lambda off: t_copy(0, tap, off).start())
-
-    load_work(first, 0)
-    sweep(work, inv, solved, root_b.at[pl.ds(0, P_SIZE)])
-    changes.finish()
+    sweep(work, inv, solved, root_b.at[pl.ds(0, P_SIZE)], SPLIT)
 
     def weights():
         return lax.dot_general(
@@ -406,13 +407,13 @@
 
     load_work(second, 1)
     own_w = wts[pl.ds(pl.multiple_of(mi * own, own), own), :]
+    sweep(work, inv, solved, root_b.at[pl.ds(P_SIZE, P_SIZE)], 0, SPLIT_2)
     each(1, n_mem, lambda off: t_wait(0, tap, off))
     for mem in range(n_mem):
         at = slice(mem * part_rows, (mem + 1) * part_rows)
         moved = jnp.dot(own_w, tap[mem], preferred_element_type=F32)
         out[:, at] = (state[:, at].astype(F32) - moved).astype(BF16)
-
-    sweep(work, inv, solved, root_b.at[pl.ds(P_SIZE, P_SIZE)])
+    sweep(work, inv, solved, root_b.at[pl.ds(P_SIZE, P_SIZE)], SPLIT_2)
     wts[...] = weights().astype(BF16)
     own_w = wts[pl.ds(pl.multiple_of(mi * own, own), own), :]
 
@@ -434,9 +435,9 @@
     own, rows = state.shape
     n = n_slab * n_sub
     total = n * n_mem
-    owners = min(n, 8)
+    owners = min(n, 4)
     chunk = P_SIZE // owners
-    c_owners = min(total, 16)
+    c_owners = min(total, 8)
     c_chunk = P_SIZE // c_owners
     n_obs = BATCHES * P_SIZE
     part_rows = rows // n_mem

time: 40.4 us -> 38.2 us (0.946)
  Pallas kernels: 37.6 us -> 35.4 us
    pallas_call x1, Pallas kernels: 37.6 us -> 35.4 us  [on_device(): pl.pallas_call(functools.partial(kernel, shape), out_shape=jax.ShapeDtype...]
where the time goes in v3:
time: 38.2 us; the launch traced here: 38 us
  Pallas kernels  35.4 us (93%)
  local copies, waits for them, and re-layouts  2.57 us (7%)
    pallas_call x1, Pallas kernels, on_device(): pl.pallas_call(functools.partial(kernel, shape), out_shape=jax.ShapeDtype...  35.4 us
    unnamed x13, local copies, waits for them, and re-layouts  2.57 us

profile of v3, /device:TPU:0, one launch (start us, length us, event | category | flops | bytes accessed | tf_op | source)
XLA Modules:
  0.0 38.0 jit_solution(11001086059521267529)
XLA Ops:
  0.0 0.0 copy-start.4
  0.0 0.0 copy-start.5
  0.0 0.0 copy-start.2
  0.0 0.0 copy-start.3
  0.0 0.0 copy-start.1
  0.0 0.7 %copy-done.4 = s32[256]{0:T(256)S(1)} copy-done((s32[256]{0:T(256)S(1)}, s32[256]{0:T(256)}, u32[]{:S(2)}) %copy-start.4) | copy-done | bytes 1048
  0.7 0.0 copy-done.5
  0.7 0.0 copy-done.2
  0.7 0.0 copy-done.3
  0.7 0.0 copy-done.1
  0.7 0.0 copy-start
  0.7 1.0 %copy-done = bf16[128,2048]{1,0:T(8,128)(2,1)S(1)} copy-done((bf16[128,2048]{1,0:T(8,128)(2,1)S(1)}, bf16[128,2048]{1,0:T(8,128)(2,1)}, u32[]{:S(2)}) %copy-start) | copy-done | bytes 524312
  1.8 35.4 %shard_map.64 = bf16[128,2048]{1,0:T(8,128)(2,1)S(1)} custom-call(bf16[128,2048]{1,0:T(8,128)(2,1)S(1)} %copy-done, s32[1,256]{1,0:T(1,128)S(1)} %bitcast.5, s32[1,256]{1,0:T(1,128)S(1)} %bitcast.6, s32[1,256]{1,0:T(1,128)S(1)} %bitcast.7, s32[1,256]{1,0:T(1,128)S(1)} %bitcast.8, f32[1,256]{1,0:T(1,128)S(1)} %bitcast.9), custom_call_target="tpu_custom_call" | custom-call | tf_op jit(solution)/shard_map/pallas_call | solution.py:446
  37.2 0.8 %copy.8 = bf16[128,2048]{1,0:T(8,128)(2,1)} copy(bf16[128,2048]{1,0:T(8,128)(2,1)S(1)} %shard_map.64) | data formatting | bytes 1048576
Async XLA Ops:
  0.0 0.7 %copy-start.4 = (s32[256]{0:T(256)S(1)}, s32[256]{0:T(256)}, u32[]{:S(2)}) copy-start(s32[256]{0:T(256)} %param.10) | copy-start | bytes 3076
  0.0 0.7 %copy-start.5 = (f32[256]{0:T(256)S(1)}, f32[256]{0:T(256)}, u32[]{:S(2)}) copy-start(f32[256]{0:T(256)} %param.11) | copy-start | bytes 3076
  0.0 0.7 %copy-start.2 = (s32[256]{0:T(256)S(1)}, s32[256]{0:T(256)}, u32[]{:S(2)}) copy-start(s32[256]{0:T(256)} %param.8) | copy-start | bytes 3076
  0.0 0.7 %copy-start.3 = (s32[256]{0:T(256)S(1)}, s32[256]{0:T(256)}, u32[]{:S(2)}) copy-start(s32[256]{0:T(256)} %param.9) | copy-start | bytes 3076
  0.0 0.7 %copy-start.1 = (s32[256]{0:T(256)S(1)}, s32[256]{0:T(256)}, u32[]{:S(2)}) copy-start(s32[256]{0:T(256)} %param.7) | copy-start | bytes 3076
  0.7 1.0 %copy-start = (bf16[128,2048]{1,0:T(8,128)(2,1)S(1)}, bf16[128,2048]{1,0:T(8,128)(2,1)}, u32[]{:S(2)}) copy-start(bf16[128,2048]{1,0:T(8,128)(2,1)} %state_hbm.1) | copy-start | bytes 1572868

commit v4 on v3

--- a/solution.py
+++ b/solution.py
@@ -417,9 +417,11 @@
     wts[...] = weights().astype(BF16)
     own_w = wts[pl.ds(pl.multiple_of(mi * own, own), own), :]
 
-    each(1, n_mem, lambda off: t_wait(1, tap1, off))
-    for mem in range(n_mem):
-        at = slice(mem * part_rows, (mem + 1) * part_rows)
+    for off in range(n_mem):
+        if off:
+            t_wait(1, tap1, off)
+        mem = lax.rem(mi + off, n_mem)
+        at = rows_of(mem)
         moved = jnp.dot(own_w, tap1[mem], preferred_element_type=F32)
         out[:, at] = (out[:, at].astype(F32) - moved).astype(BF16)
 

time: 38.2 us -> 38 us (level)
  no operation moved by 1% of the time
where the time goes in v4:
time: 38 us; the launch traced here: 37.9 us
  Pallas kernels  35.3 us (93%)
  local copies, waits for them, and re-layouts  2.57 us (7%)
    pallas_call x1, Pallas kernels, on_device(): pl.pallas_call(functools.partial(kernel, shape), out_shape=jax.ShapeDtype...  35.3 us
    unnamed x13, local copies, waits for them, and re-layouts  2.57 us

profile of v4, /device:TPU:0, one launch (start us, length us, event | category | flops | bytes accessed | tf_op | source)
XLA Modules:
  0.0 37.9 jit_solution(2183603980142455138)
XLA Ops:
  0.0 0.0 copy-start.4
  0.0 0.0 copy-start.5
  0.0 0.0 copy-start.2
  0.0 0.0 copy-start.3
  0.0 0.0 copy-start.1
  0.0 0.7 %copy-done.4 = s32[256]{0:T(256)S(1)} copy-done((s32[256]{0:T(256)S(1)}, s32[256]{0:T(256)}, u32[]{:S(2)}) %copy-start.4) | copy-done | bytes 1048
  0.7 0.0 copy-done.5
  0.7 0.0 copy-done.2
  0.7 0.0 copy-done.3
  0.7 0.0 copy-done.1
  0.7 0.0 copy-start
  0.7 1.0 %copy-done = bf16[128,2048]{1,0:T(8,128)(2,1)S(1)} copy-done((bf16[128,2048]{1,0:T(8,128)(2,1)S(1)}, bf16[128,2048]{1,0:T(8,128)(2,1)}, u32[]{:S(2)}) %copy-start) | copy-done | bytes 524312
  1.8 35.3 %shard_map.64 = bf16[128,2048]{1,0:T(8,128)(2,1)S(1)} custom-call(bf16[128,2048]{1,0:T(8,128)(2,1)S(1)} %copy-done, s32[1,256]{1,0:T(1,128)S(1)} %bitcast.5, s32[1,256]{1,0:T(1,128)S(1)} %bitcast.6, s32[1,256]{1,0:T(1,128)S(1)} %bitcast.7, s32[1,256]{1,0:T(1,128)S(1)} %bitcast.8, f32[1,256]{1,0:T(1,128)S(1)} %bitcast.9), custom_call_target="tpu_custom_call" | custom-call | tf_op jit(solution)/shard_map/pallas_call | solution.py:448
  37.1 0.8 %copy.8 = bf16[128,2048]{1,0:T(8,128)(2,1)} copy(bf16[128,2048]{1,0:T(8,128)(2,1)S(1)} %shard_map.64) | data formatting | bytes 1048576
Async XLA Ops:
  0.0 0.7 %copy-start.4 = (s32[256]{0:T(256)S(1)}, s32[256]{0:T(256)}, u32[]{:S(2)}) copy-start(s32[256]{0:T(256)} %param.10) | copy-start | bytes 3076
  0.0 0.7 %copy-start.5 = (f32[256]{0:T(256)S(1)}, f32[256]{0:T(256)}, u32[]{:S(2)}) copy-start(f32[256]{0:T(256)} %param.11) | copy-start | bytes 3076
  0.0 0.7 %copy-start.2 = (s32[256]{0:T(256)S(1)}, s32[256]{0:T(256)}, u32[]{:S(2)}) copy-start(s32[256]{0:T(256)} %param.8) | copy-start | bytes 3076
  0.0 0.7 %copy-start.3 = (s32[256]{0:T(256)S(1)}, s32[256]{0:T(256)}, u32[]{:S(2)}) copy-start(s32[256]{0:T(256)} %param.9) | copy-start | bytes 3076
  0.0 0.7 %copy-start.1 = (s32[256]{0:T(256)S(1)}, s32[256]{0:T(256)}, u32[]{:S(2)}) copy-start(s32[256]{0:T(256)} %param.7) | copy-start | bytes 3076
  0.7 1.0 %copy-start = (bf16[128,2048]{1,0:T(8,128)(2,1)S(1)}, bf16[128,2048]{1,0:T(8,128)(2,1)}, u32[]{:S(2)}) copy-start(bf16[128,2048]{1,0:T(8,128)(2,1)} %state_hbm.1) | copy-start | bytes 1572868
